TPU v7x, 256 devices: a whole 4x4x8 slice. The times are simulated.
256 devices in a mesh: fam: 8 (over y_hi, x), owner: 32 (over y_lo, z, core).
Axes of the slice: x: 4, y: 4 (y_hi: 2, y_lo: 2; y = y_hi * 2 + y_lo), z: 8, core: 2. Of those that a mesh axis runs over, the one named last changes fastest.
Arguments:
- wavefunction: bfloat16 [16384, 512], P('owner'), may hold values from -6 to 6
- left_blocks: bfloat16 [8, 8, 16384, 1024], P('fam', None, 'owner'), may hold values from -0.1875 to 0.1875
- right_blocks: bfloat16 [8, 512, 512], P('fam'), may hold values from -0.0625 to 0.0625
- term_sources: int32 [8, 16, 8], replicated, may hold values from 0 to 15
- term_counts: int32 [8, 16], replicated, may hold values from 1 to 8, as said below
- sector_rows: int32 [16], replicated, may hold values from 256 to 1024
Outputs:
- sigma: bfloat16 [16384, 512], P('owner', 'fam')
Inputs may be any that keep to these rules, and one draw needn't show every extreme that they name: `term_counts`: every entry lies in 1 to 8; for every output sector some family has exactly 8 live slots.
All inputs are finite; a program needn't handle non-finite values.
Results may differ from a plain program's by a relative error of at most 0.0095.
Values may be sent and summed in bfloat16 or wider, within the bound.
A program may use at most 128 MiB of HBM per device.

v0:
```python
import jax
import jax.numpy as jnp
from jax import lax
from jax.sharding import PartitionSpec as P


def in_blocks(value, dim, count):
    dims = value.shape
    parts = value.reshape(*dims[:dim], count, dims[dim] // count, *dims[dim + 1 :])
    return jnp.moveaxis(parts, dim, 0)


def sent_and_summed(value, axis, dim):
    count = lax.axis_size(axis)
    parts = lax.all_to_all(in_blocks(value, dim, count), axis, 0, 0, tiled=True)
    return jnp.sum(parts, axis=0)


def row_keep(global_rows, sector_len, sector_rows):
    sector = global_rows // sector_len
    table = jnp.arange(sector_rows.shape[0], dtype=jnp.int32)
    used = jnp.sum(jnp.where(sector[:, None] == table[None, :], sector_rows[None, :], 0), axis=1)
    return global_rows % sector_len < used


def body(wavefunction, left_blocks, right_blocks, term_sources, term_counts, sector_rows):
    rows_dev, columns = wavefunction.shape
    slot_count = left_blocks.shape[1]
    sector_len = left_blocks.shape[3]
    fam_here = lax.axis_index("fam")
    first_row = lax.axis_index("owner") * rows_dev
    global_rows = first_row + jnp.arange(rows_dev, dtype=jnp.int32)
    keep = row_keep(global_rows, sector_len, sector_rows)
    masked = jnp.where(keep[:, None], wavefunction, jnp.zeros_like(wavefunction))
    out_sector = [(first_row + 0) // sector_len]
    slot_ids = jnp.arange(slot_count, dtype=jnp.int32)
    items = left_blocks[0]
    right_stack = right_blocks[0]
    block = 0
    live = [slot_ids < term_counts[fam_here, out_sector[block]]]
    source = term_sources[fam_here, out_sector[block], slot_ids]
    whole = lax.all_gather(masked, "owner", axis=0, tiled=True)
    stacked = whole.reshape(whole.shape[0] // sector_len, sector_len, whole.shape[1])
    sources = jnp.take(stacked, source, axis=0)
    accum = jnp.stack(
        [jnp.einsum("kri,kic->krc", items, sources, preferred_element_type=jnp.float32)], axis=0
    )
    partial_value = accum.astype(jnp.bfloat16)
    block = 0
    used = jnp.where(
        live[block][:, None, None], partial_value[block], jnp.zeros_like(partial_value[block])
    )
    total = jnp.einsum("krc,cd->rd", used, right_stack, preferred_element_type=jnp.float32)
    combined = total
    combined = jnp.where(keep[:, None], combined, jnp.zeros_like(combined))
    summed = sent_and_summed(combined, "fam", 1)
    return summed.astype(jnp.bfloat16)


def solution(mesh):
    return jax.shard_map(
        body,
        mesh=mesh,
        in_specs=(
            P("owner", None),
            P("fam", None, "owner", None),
            P("fam", None, None),
            P(),
            P(),
            P(),
        ),
        out_specs=P("owner", "fam"),
        check_vma=False,
    )
```

profile of v0, /device:TPU:1, one launch (start us, length us, event | category | flops | bytes accessed | tf_op | source)
XLA Modules:
  0.0 180.4 jit_solution(4787722068686721112)
XLA Ops:
  6.5 0.0 copy-start
  6.5 0.0 all-gather.2.cloned.1.call-start
  6.5 1.3 copy.10
  7.9 0.7 select_reduce_fusion
  8.6 0.8 broadcast_select_fusion
  9.5 0.0 all-gather.2.cloned.1.call-update
  9.5 1.3 dynamic_slice.3
  10.8 1.4 gather_fusion
  12.2 0.7 compare_and_fusion
  12.9 100.7 %all-gather.2.cloned.1.call-done = bf16[16384,512]{0,1:T(8,128)(2,1)} async-done(((bf16[512,512]{0,1:T(8,128)(2,1)}), bf16[16384,512]{0,1:T(8,128)(2,1)}) %all-gather.2.cloned.1.call-update) | async-done | bytes 16777232 | tf_op jit(solution)/shard_map/all_gather | solution.py:42
  113.6 14.0 %copy.14 = bf16[64,16,8,1024]{3,2,0,1:T(8,128)(2,1)} copy(bf16[64,16,8,1024]{3,2,1,0:T(8,128)(2,1)} %bitcast.24) | data formatting | bytes 33554432 | tf_op jit(solution)/shard_map/reshape | solution.py:43
  127.6 10.4 %gather_fusion.1 = bf16[8,1024,512]{1,2,0:T(8,128)(2,1)} fusion(bf16[16,1024,512]{1,2,0:T(8,128)(2,1)} %bitcast.23, s32[1024]{0:T(1024)S(1)} %pad_clamp_fusion), kind=kCustom, calls=%fused_computation.1 | custom fusion | bytes 16777248 | tf_op jit(solution)/shard_map/jit(_take)/gather | solution.py:44
  138.1 10.7 %convert_reduce_fusion = bf16[512,512]{1,0:T(8,128)(2,1)S(1)} fusion(pred[8]{0:T(512)(128)(4,1)S(1)} %get-tuple-element.6, bf16[1,8,512,1024]{3,2,1,0:T(8,128)(2,1)} %param.7, bf16[8,1024,512]{1,2,0:T(8,128)(2,1)} %gather_fusion.1, pred[8]{0:T(512)(128)(4,1)S(1)} %get-tuple-element.5), kind=kOutput, calls=%fused_computation.5 | convolution fusion | flops 4307288064 | bytes 17301520 | tf_op jit(solution)/shard_map/kri,kic->krc/dot_general | solution.py:46
  148.8 0.0 copy-done
  148.8 0.5 convolution_select_fusion
  149.3 23.6 %all_to_all.5 = f32[8,512,64]{1,2,0:T(8,128)S(1)} all-to-all(f32[8,512,64]{1,2,0:T(8,128)S(1)} %bitcast.25), channel_id=1, replica_groups=mesh['fam'=8,'owner'=32] {'fam'}, dimensions={0} | all-to-all | bytes 2097152 | tf_op jit(solution)/shard_map/all_to_all | solution.py:15
  172.9 0.7 reduce_sum.29
  (5 shorter events, 0.0 us)
Async XLA Ops:
  6.5 142.3 %copy-start = (bf16[1,512,512]{2,1,0:T(8,128)(2,1)S(1)}, bf16[1,512,512]{2,1,0:T(8,128)(2,1)}, u32[]{:S(2)}) copy-start(bf16[1,512,512]{2,1,0:T(8,128)(2,1)} %param.8) | copy-start | bytes 1572868
  6.5 107.1 %all-gather.2.cloned.1.call-start = ((), (), s32[]{:S(2)}) async-start(), calls=%async_computation.1 | async-start | bytes 17301504 | tf_op jit(solution)/shard_map/all_gather | solution.py:42
Sparse Core Ops, SparseCore 0:
  9.6 103.9 all-gather.1
where the time goes:
time: 181 us; the launch traced here: 180 us
  waiting for transfers between devices  101 us (56%)
  local copies, waits for them, and re-layouts  28.4 us (16%)
  blocking collectives  23.6 us (13%)
  between operations  13.5 us (7%)
  matrix products  11.2 us (6%)
  other arithmetic  2.99 us (2%)
    all_gather x1, waiting for transfers between devices, body(): whole = lax.all_gather(masked, 'owner', axis=0, tiled=True)  101 us
    all_to_all x1, blocking collectives, sent_and_summed(): parts = lax.all_to_all(in_blocks(value, dim, count), axis, 0, 0, tiled=True)  23.6 us
    reshape x1, local copies, waits for them, and re-layouts, body(): whole.reshape(whole.shape[0] // sector_len, sector_len, whole.shape[1])  14 us
    dot_general x1, matrix products, body(): jnp.einsum('kri,kic->krc', items, sources, preferred_element_type=jnp.flo...  10.7 us
    gather x1, local copies, waits for them, and re-layouts, body(): sources = jnp.take(stacked, source, axis=0)  10.4 us
  transfers between devices with their start and end apart: 1, of which 1 were waited for; matrix products, arithmetic and copies ran while one was open for 2% of the time, Pallas kernels for 0%

commit v1 on v0

--- a/solution.py
+++ b/solution.py
@@ -39,7 +39,9 @@
     block = 0
     live = [slot_ids < term_counts[fam_here, out_sector[block]]]
     source = term_sources[fam_here, out_sector[block], slot_ids]
-    whole = lax.all_gather(masked, "owner", axis=0, tiled=True)
+    whole = jnp.concatenate(
+        lax.all_to_all(jnp.stack([masked] * lax.axis_size("owner")), "owner", 0, 0), axis=0
+    )
     stacked = whole.reshape(whole.shape[0] // sector_len, sector_len, whole.shape[1])
     sources = jnp.take(stacked, source, axis=0)
     accum = jnp.stack(

time: 181 us -> 436 us (2.41)
  the two profiles are of different devices: /device:TPU:1 before, /device:TPU:96 now
where the time goes in v1:
time: 436 us
  waiting for transfers between devices  371 us (85%)
  blocking collectives  23.4 us (5%)
  local copies, waits for them, and re-layouts  19.9 us (5%)
  matrix products  10.7 us (2%)
  starting transfers between devices  9.02 us (2%)
    all_to_all x1, waiting for transfers between devices, body(): lax.all_to_all(jnp.stack([masked] * lax.axis_size('owner')), 'owner', 0, 0)  371 us
    all_to_all x1, blocking collectives, sent_and_summed(): parts = lax.all_to_all(in_blocks(value, dim, count), axis, 0, 0, tiled=True)  23.4 us
    gather x1, local copies, waits for them, and re-layouts, body(): sources = jnp.take(stacked, source, axis=0)  10.4 us
    dot_general x1, matrix products, body(): jnp.einsum('kri,kic->krc', items, sources, preferred_element_type=jnp.flo...  10.2 us
    all_to_all x1, starting transfers between devices, body(): lax.all_to_all(jnp.stack([masked] * lax.axis_size('owner')), 'owner', 0, 0)  9.02 us
  transfers between devices with their start and end apart: 1, of which 1 were waited for; matrix products, arithmetic and copies ran while one was open for 1% of the time, Pallas kernels for 0%

profile of v1, /device:TPU:96, one launch (start us, length us, event | category | flops | bytes accessed | tf_op | source)
XLA Modules:
  0.0 435.9 jit_solution(16040021069954372621)
XLA Ops:
  0.0 0.0 copy-start
  0.0 1.3 copy.13
  1.3 0.7 select_reduce_fusion
  2.1 0.2 copy.14
  2.4 6.0 %stack.2 = bf16[32,512,512]{2,1,0:T(8,128)(2,1)} broadcast(bf16[512,512]{1,0:T(8,128)(2,1)S(1)} %copy.14), dimensions={1,2} | broadcast | bytes 17301504 | tf_op jit(solution)/shard_map/stack | solution.py:43
  8.3 0.0 copy-start.1
  8.3 9.0 %all-to-all-start = ((bf16[32,512,512]{2,1,0:T(8,128)(2,1)}), bf16[32,512,512]{2,1,0:T(8,128)(2,1)}, u32[]{:S(2)}, u32[]{:S(2)}) async-start(bf16[32,512,512]{2,1,0:T(8,128)(2,1)} %stack.2), calls=%async_computation | async-start | bytes 33554432 | tf_op jit(solution)/shard_map/all_to_all | solution.py:43
  17.4 1.3 dynamic_slice.3
  18.7 0.0 copy-done.1
  18.7 0.6 gather_fusion
  19.3 0.7 compare_and_fusion
  20.0 370.6 %all-to-all-done = bf16[32,512,512]{2,1,0:T(8,128)(2,1)} async-done(((bf16[32,512,512]{2,1,0:T(8,128)(2,1)}), bf16[32,512,512]{2,1,0:T(8,128)(2,1)}, u32[]{:S(2)}, u32[]{:S(2)}) %all-to-all-start) | async-done | bytes 16777248 | tf_op jit(solution)/shard_map/all_to_all | solution.py:43
  390.6 10.4 %gather_fusion.1 = bf16[8,1024,512]{2,1,0:T(8,128)(2,1)} fusion(bf16[16,1024,512]{2,1,0:T(8,128)(2,1)} %bitcast.2, s32[1024]{0:T(1024)S(1)} %pad_clamp_fusion), kind=kCustom, calls=%fused_computation.1 | custom fusion | bytes 16777248 | tf_op jit(solution)/shard_map/jit(_take)/gather | solution.py:46
  401.0 10.2 %convert_reduce_fusion = bf16[512,512]{1,0:T(8,128)(2,1)S(1)} fusion(pred[8]{0:T(512)(128)(4,1)S(1)} %get-tuple-element.6, bf16[1,8,512,1024]{3,2,1,0:T(8,128)(2,1)} %param.7, bf16[8,1024,512]{2,1,0:T(8,128)(2,1)} %gather_fusion.1, pred[8]{0:T(512)(128)(4,1)S(1)} %get-tuple-element.5), kind=kOutput, calls=%fused_computation.4 | convolution fusion | flops 4307288064 | bytes 17301520 | tf_op jit(solution)/shard_map/kri,kic->krc/dot_general | solution.py:48
  411.2 0.0 copy-done
  411.2 0.5 convolution_select_fusion
  411.7 23.4 %all_to_all.10 = f32[8,512,64]{1,2,0:T(8,128)S(1)} all-to-all(f32[8,512,64]{1,2,0:T(8,128)S(1)} %bitcast.20), channel_id=1, replica_groups=mesh['fam'=8,'owner'=32] {'fam'}, dimensions={0} | all-to-all | bytes 2097152 | tf_op jit(solution)/shard_map/all_to_all | solution.py:15
  435.2 0.7 reduce_sum.29
  (6 shorter events, 0.1 us)
Async XLA Ops:
  0.0 411.2 %copy-start = (bf16[1,512,512]{2,1,0:T(8,128)(2,1)S(1)}, bf16[1,512,512]{2,1,0:T(8,128)(2,1)}, u32[]{:S(2)}) copy-start(bf16[1,512,512]{2,1,0:T(8,128)(2,1)} %param.8) | copy-start | bytes 1572868
  8.3 10.3 %copy-start.1 = (s32[8,16,8]{1,2,0:T(8,128)S(1)}, s32[8,16,8]{1,2,0:T(8,128)}, u32[]{:S(2)}) copy-start(s32[8,16,8]{1,2,0:T(8,128)} %param.9) | copy-start | bytes 12292
  8.3 382.2 %all-to-all-start = ((bf16[32,512,512]{2,1,0:T(8,128)(2,1)}), bf16[32,512,512]{2,1,0:T(8,128)(2,1)}, u32[]{:S(2)}, u32[]{:S(2)}) async-start(bf16[32,512,512]{2,1,0:T(8,128)(2,1)} %stack.2), calls=%async_computation | async-start | bytes 33554432 | tf_op jit(solution)/shard_map/all_to_all | solution.py:43
